TPU v7x, 32 devices: a whole 2x2x4 slice. The times are simulated.
32 devices in a mesh: groups: 2 (over y), tiles: 4 (over z), chan: 2 (over x), sub: 2 (over core).
Axes of the slice: x: 2, y: 2, z: 4, core: 2. Of those that a mesh axis runs over, the one named last changes fastest.
Arguments:
- features: bfloat16 [128, 256, 256], P(('groups', 'tiles', 'sub'), 'chan'), parts along dimension 0, may hold values from -6 to 6
- cotangent: bfloat16 [128, 256, 256], P(('groups', 'tiles', 'sub'), 'chan'), parts along dimension 0, may hold values from -6 to 6
- down_factor: bfloat16 [2, 256, 64], P(None, 'chan'), may hold values from -0.375 to 0.375
- core_kernel: bfloat16 [2, 9, 64, 64], replicated, may hold values from -0.25 to 0.25
- up_factor: bfloat16 [2, 256, 64], P(None, 'chan'), may hold values from -0.75 to 0.75
- tile_count: int32 [16], P(('groups', 'tiles', 'sub')), parts along dimension 0, may hold values from 4 to 8, as said below
- neighbour_owner: int32 [128, 8], P(('groups', 'tiles', 'sub')), parts along dimension 0, may hold values from -1 to 7, as said below
- neighbour_slot: int32 [128, 8], P(('groups', 'tiles', 'sub')), parts along dimension 0, may hold values from -1 to 7, as said below
Outputs:
- input_gradient: bfloat16 [128, 256, 256], P(('groups', 'tiles', 'sub'), 'chan'), parts along dimension 0
- down_gradient: float32 [4, 256, 64], P('groups', 'chan'), parts along dimension 0
- core_gradient: float32 [4, 9, 64, 64], P('groups', None, 'chan'), parts along dimension 0
- up_gradient: float32 [4, 256, 64], P('groups', 'chan'), parts along dimension 0
There are 2 independent parts, one for each index of `groups`. A program takes and returns all parts, laid end to end along the dimension named above; an argument that names none is the same for every part. Nothing has to cross between parts.
Inputs may be any that keep to these rules, and one draw needn't show every extreme that they name: `tile_count`: every count is even; some device holds exactly 8 live tiles and some exactly 4. `neighbour_owner`: -1 where the slot is not live or no tissue tile lies in that direction. Otherwise the owner is the slot's own device or the device just before or after it along the owners, and the named slot is live there. Neighbourhood is mutual: if tile h lies in some direction of tile g, then g lies in the opposite direction of h. `neighbour_slot`: -1 exactly where neighbour_owner is -1.
All inputs are finite; a program needn't handle non-finite values.
Results may differ from a plain program's by a relative error of at most 0.014.
Values may be sent and summed in bfloat16 or wider, within the bound.
A program may use at most 64 MiB of HBM per device.

v0:
```python
import jax
import jax.numpy as jnp
from jax import lax
from jax.sharding import PartitionSpec as P

TILE = 16
LAYERS = 2
EDGE_ROWS = [1, 6, 3, 4]
EDGE_PIECES = [1, 0, 3, 2]
CORNER_ROWS = [0, 2, 5, 7]
CORNER_PIECES = [3, 2, 1, 0]


def padded_2(cells, sides, width):
    for axis, dim in sides:
        count = lax.axis_size(axis)
        ends = count - 1
        head = lax.slice_in_dim(cells, 0, width, axis=dim)
        tail = lax.slice_in_dim(cells, cells.shape[dim] - width, cells.shape[dim], axis=dim)
        cells = jnp.concatenate(
            [
                lax.ppermute(tail, axis, [(i, (i + 1) % count) for i in range(ends)]),
                cells,
                lax.ppermute(head, axis, [((i + 1) % count, i) for i in range(ends)]),
            ],
            axis=dim,
        )
    return cells


def cycle_of(squares):
    edge_cells = jnp.concatenate(
        [squares[:, :, 0, :], squares[:, :, -1, :], squares[:, :, :, 0], squares[:, :, :, -1]],
        axis=2,
    )
    corners = jnp.stack(
        [squares[:, :, 0, 0], squares[:, :, 0, -1], squares[:, :, -1, 0], squares[:, :, -1, -1]],
        axis=2,
    )
    return jnp.concatenate([edge_cells, corners], axis=2)


def assemble(squares, side_cells, corner_cells):
    top_row = jnp.concatenate(
        [corner_cells[0][:, :, None], side_cells[0], corner_cells[1][:, :, None]], axis=2
    )
    bottom_row = jnp.concatenate(
        [corner_cells[2][:, :, None], side_cells[1], corner_cells[3][:, :, None]], axis=2
    )
    middle = jnp.concatenate(
        [side_cells[2][:, :, :, None], squares, side_cells[3][:, :, :, None]], axis=3
    )
    return jnp.concatenate([top_row[:, :, None, :], middle, bottom_row[:, :, None, :]], axis=2)


def selectors(neighbour_owner, neighbour_slot, device_here, slot_total):
    local_row = (neighbour_owner - device_here + 1) * slot_total + neighbour_slot
    columns = jnp.arange(3 * slot_total)
    matched = (local_row[:, :, None] == columns[None, None, :]) & (neighbour_owner[:, :, None] >= 0)
    return matched.astype(jnp.bfloat16)


def place_border(flat_cells, extended, chooser):
    squares = flat_cells.reshape(flat_cells.shape[0], flat_cells.shape[1], TILE, TILE)
    nearest = jnp.einsum(
        "uvd,dck->uvck",
        jnp.stack([chooser[:, row] for row in EDGE_ROWS], axis=1),
        extended[:, :, : 4 * TILE],
        preferred_element_type=jnp.float32,
    ).astype(jnp.bfloat16)
    diagonal = jnp.einsum(
        "uvd,dck->uvck",
        jnp.stack([chooser[:, row] for row in CORNER_ROWS], axis=1),
        extended[:, :, 4 * TILE :],
        preferred_element_type=jnp.float32,
    ).astype(jnp.bfloat16)
    side_cells = [
        nearest[:, which_side, :, piece_index * TILE : (piece_index + 1) * TILE]
        for which_side, piece_index in enumerate(EDGE_PIECES)
    ]
    corner_cells = [
        diagonal[:, which_side, :, piece_index]
        for which_side, piece_index in enumerate(CORNER_PIECES)
    ]
    return assemble(squares, side_cells, corner_cells)


def window(padded, shift_rows, shift_cols):
    section = padded[:, :, shift_rows : shift_rows + TILE, shift_cols : shift_cols + TILE]
    return section.reshape(section.shape[0], section.shape[1], TILE * TILE)


def stacked_windows(padded, flipped):
    if flipped:
        return jnp.stack(
            [window(padded, 2 - offset // 3, 2 - offset % 3) for offset in range(9)], axis=0
        )
    return jnp.stack([window(padded, offset // 3, offset % 3) for offset in range(9)], axis=0)


def forward_conv(windows, kernel):
    return jnp.einsum("tsr,turq->usq", kernel, windows, preferred_element_type=jnp.float32)


def backward_conv(padded, kernel):
    return jnp.einsum(
        "tsr,tusq->urq", kernel, stacked_windows(padded, True), preferred_element_type=jnp.float32
    )


def core_gradient_of(gradient, windows):
    return jnp.einsum("usq,turq->tsr", gradient, windows, preferred_element_type=jnp.float32)


def blocked_product(factor, data, members):
    width = factor.shape[0] // members
    running = jnp.zeros((data.shape[0], factor.shape[1], data.shape[2]), jnp.float32)
    for member in range(members):
        partial_value = jnp.einsum(
            "cr,ucq->urq",
            factor[member * width : (member + 1) * width],
            data[:, member * width : (member + 1) * width],
            preferred_element_type=jnp.float32,
        )
        running = running + lax.optimization_barrier(partial_value.astype(jnp.bfloat16)).astype(
            jnp.float32
        )
    return running.astype(jnp.bfloat16)


def settle(down_part, core_part, up_part):
    return (down_part, core_part, up_part)


def whole_tiles(
    features,
    cotangent,
    down_factor,
    core_kernel,
    up_factor,
    tile_count,
    neighbour_owner,
    neighbour_slot,
):
    slot_total = features.shape[0]
    members = lax.axis_size("chan")
    rows_here = slot_total // members
    device_here = lax.axis_index(("tiles", "sub"))
    first_slot = lax.axis_index("chan") * rows_here
    hidden, upstream = (
        lax.all_to_all(features, "chan", split_axis=0, concat_axis=1, tiled=True),
        lax.all_to_all(cotangent, "chan", split_axis=0, concat_axis=1, tiled=True),
    )
    alive = (first_slot + jnp.arange(rows_here) < tile_count[0]).astype(jnp.bfloat16)
    hidden = hidden * alive[:, None, None]
    upstream = upstream * alive[:, None, None]
    down_whole, up_whole = (
        lax.all_gather(down_factor, "chan", axis=1, tiled=True),
        lax.all_gather(up_factor, "chan", axis=1, tiled=True),
    )
    near_owner = lax.dynamic_slice_in_dim(neighbour_owner, first_slot, rows_here, 0)
    near_slot = lax.dynamic_slice_in_dim(neighbour_slot, first_slot, rows_here, 0)
    chooser = selectors(near_owner, near_slot, device_here, slot_total)

    def padded_of(cells):
        border = cycle_of(cells.reshape(rows_here, cells.shape[1], TILE, TILE))
        owner_cycle = lax.all_gather(border, "chan", axis=0, tiled=True)
        extended = padded_2(owner_cycle, ((("tiles", "sub"), 0),), slot_total)
        return place_border(cells, extended, chooser)

    saved_layers = []
    for layer_index in range(LAYERS):
        activations = blocked_product(down_whole[layer_index], hidden, members)
        windows = stacked_windows(padded_of(activations), False)
        mixed = forward_conv(windows, core_kernel[layer_index]).astype(jnp.bfloat16)
        preact = jnp.einsum(
            "cs,usq->ucq", up_whole[layer_index], mixed, preferred_element_type=jnp.float32
        )
        saved_layers.append((hidden, windows, mixed, preact))
        hidden = (hidden.astype(jnp.float32) + jax.nn.silu(preact)).astype(jnp.bfloat16)
    down_list = [None] * LAYERS
    core_list = [None] * LAYERS
    up_list = [None] * LAYERS
    for layer_index in reversed(range(LAYERS)):
        hidden, windows, mixed, preact = saved_layers[layer_index]
        squashed = jax.nn.sigmoid(preact)
        pre_gradient = (
            upstream.astype(jnp.float32) * squashed * (1.0 + preact * (1.0 - squashed))
        ).astype(jnp.bfloat16)
        up_part = jnp.einsum("ucq,usq->cs", pre_gradient, mixed, preferred_element_type=jnp.float32)
        mixed_gradient = blocked_product(up_whole[layer_index], pre_gradient, members)
        core_part = core_gradient_of(mixed_gradient, windows)
        gradient_padded = padded_of(mixed_gradient)
        act_gradient = backward_conv(gradient_padded, core_kernel[layer_index]).astype(jnp.bfloat16)
        down_part = jnp.einsum(
            "ucq,urq->cr", hidden, act_gradient, preferred_element_type=jnp.float32
        )
        through = jnp.einsum(
            "cr,urq->ucq", down_whole[layer_index], act_gradient, preferred_element_type=jnp.float32
        )
        upstream = (upstream.astype(jnp.float32) + through).astype(jnp.bfloat16)
        down_part, up_part = (
            lax.psum_scatter(
                down_part.astype(jnp.bfloat16), "chan", scatter_dimension=0, tiled=True
            ).astype(jnp.float32),
            lax.psum_scatter(
                up_part.astype(jnp.bfloat16), "chan", scatter_dimension=0, tiled=True
            ).astype(jnp.float32),
        )
        core_part = lax.psum_scatter(
            core_part.astype(jnp.bfloat16), "chan", scatter_dimension=1, tiled=True
        ).astype(jnp.float32)
        down_list[layer_index], core_list[layer_index], up_list[layer_index] = settle(
            down_part, core_part, up_part
        )
    upstream = lax.all_to_all(upstream, "chan", split_axis=1, concat_axis=0, tiled=True)
    return (upstream, down_list, core_list, up_list)


def local(
    features,
    cotangent,
    down_factor,
    core_kernel,
    up_factor,
    tile_count,
    neighbour_owner,
    neighbour_slot,
):
    upstream, down_list, core_list, up_list = whole_tiles(
        features,
        cotangent,
        down_factor,
        core_kernel,
        up_factor,
        tile_count,
        neighbour_owner,
        neighbour_slot,
    )
    down_gradient = jnp.stack(down_list, axis=0)
    core_gradient = jnp.stack(core_list, axis=0)
    up_gradient = jnp.stack(up_list, axis=0)
    down_gradient, core_gradient, up_gradient = lax.psum(
        (down_gradient, core_gradient, up_gradient), ("tiles", "sub")
    )
    return (upstream, down_gradient, core_gradient, up_gradient)


def solution(mesh):
    return jax.shard_map(
        local,
        mesh=mesh,
        in_specs=(
            P(("groups", "tiles", "sub"), "chan", None),
            P(("groups", "tiles", "sub"), "chan", None),
            P(None, "chan", None),
            P(),
            P(None, "chan", None),
            P(("groups", "tiles", "sub")),
            P(("groups", "tiles", "sub"), None),
            P(("groups", "tiles", "sub"), None),
        ),
        out_specs=(
            P(("groups", "tiles", "sub"), "chan", None),
            P("groups", "chan", None),
            P("groups", None, "chan", None),
            P("groups", "chan", None),
        ),
        check_vma=False,
    )
```

profile of v0, /device:TPU:0, one launch (start us, length us, event | category | flops | bytes accessed | tf_op | source)
XLA Modules:
  0.0 318.6 jit_solution(4942004799345471863)
XLA Ops:
  7.2 4.3 %all-to-all-start.1 = ((bf16[8,128,256]{2,1,0:T(8,128)(2,1)}), bf16[8,128,256]{2,1,0:T(8,128)(2,1)S(1)}, u32[]{:S(2)}, u32[]{:S(2)}) async-start(bf16[8,128,256]{2,1,0:T(8,128)(2,1)} %param.8), calls=%async_computation.1 | async-start | bytes 1048576 | tf_op jit(solution)/shard_map/all_to_all | solution.py:151
  13.7 6.6 %all-to-all-done.1 = bf16[8,128,256]{2,1,0:T(8,128)(2,1)S(1)} async-done(((bf16[8,128,256]{2,1,0:T(8,128)(2,1)}), bf16[8,128,256]{2,1,0:T(8,128)(2,1)S(1)}, u32[]{:S(2)}, u32[]{:S(2)}) %all-to-all-start.1) | async-done | bytes 524320 | tf_op jit(solution)/shard_map/all_to_all | solution.py:151
  20.3 3.5 %all-to-all-start = ((bf16[8,128,256]{2,1,0:T(8,128)(2,1)}), bf16[8,128,256]{2,1,0:T(8,128)(2,1)S(1)}, u32[]{:S(2)}, u32[]{:S(2)}) async-start(bf16[8,128,256]{2,1,0:T(8,128)(2,1)} %param.9), calls=%async_computation | async-start | bytes 1048576 | tf_op jit(solution)/shard_map/all_to_all | solution.py:152
  23.8 8.3 %all_gather.18 = bf16[2,256,64]{1,2,0:T(8,128)(2,1)S(1)} all-gather(bf16[2,128,64]{1,2,0:T(8,128)(2,1)S(1)} %copy-done.36), channel_id=1, replica_groups=mesh['groups'=2,'tiles'=4,'chan'=2,'sub'=2] {'chan'}, dimensions={1}, use_global_device_ids=true | all-gather | bytes 98304 | tf_op jit(solution)/shard_map/all_gather | solution.py:158
  32.2 4.6 %all_gather.20 = bf16[2,256,64]{1,2,0:T(8,128)(2,1)S(1)} all-gather(bf16[2,128,64]{1,2,0:T(8,128)(2,1)S(1)} %copy-done.37), channel_id=1, replica_groups=mesh['groups'=2,'tiles'=4,'chan'=2,'sub'=2] {'chan'}, dimensions={1}, use_global_device_ids=true | all-gather | bytes 98304 | tf_op jit(solution)/shard_map/all_gather | solution.py:159
  38.7 4.9 %all_gather.19 = bf16[8,64,68]{2,1,0:T(8,128)(2,1)S(1)} all-gather(bf16[4,64,68]{2,1,0:T(8,128)(2,1)S(1)} %copy.660), channel_id=1, replica_groups=mesh['groups'=2,'tiles'=4,'chan'=2,'sub'=2] {'chan'}, dimensions={0}, use_global_device_ids=true | all-gather | bytes 104448 | tf_op jit(solution)/shard_map/all_gather | solution.py:167
  43.8 1.3 collective-permute-start.1
  45.1 3.0 collective-permute-start
  54.6 1.4 add_convert_fusion
  57.4 4.9 %all_gather.21 = bf16[8,64,68]{2,1,0:T(8,128)(2,1)S(1)} all-gather(bf16[4,64,68]{2,1,0:T(8,128)(2,1)S(1)} %copy.692), channel_id=1, replica_groups=mesh['groups'=2,'tiles'=4,'chan'=2,'sub'=2] {'chan'}, dimensions={0}, use_global_device_ids=true | all-gather | bytes 104448 | tf_op jit(solution)/shard_map/all_gather | solution.py:167
  62.5 1.3 collective-permute-start.3
  63.8 3.5 %collective-permute-start.2 = (bf16[8,64,68]{1,0,2:T(8,128)(2,1)S(1)}, bf16[8,64,68]{1,0,2:T(8,128)(2,1)S(1)}, u32[]{:S(2)}, u32[]{:S(2)}) collective-permute-start(bf16[8,64,68]{1,0,2:T(8,128)(2,1)S(1)} %copy.693), channel_id=1, source_target_pairs={{0,1},{1,4},{4,5},{5,8},{8,9},{9,12},{12,13},{2,3},{3,6},{6,7},{7,... | collective-permute-start | bytes 208904 | tf_op jit(solution)/shard_map/ppermute | solution.py:22
  72.8 1.7 copy.716
  77.0 1.7 copy.711
  89.4 1.5 concatenate.146
  91.6 5.1 %all_gather.22 = bf16[8,64,68]{2,1,0:T(8,128)(2,1)S(1)} all-gather(bf16[4,64,68]{2,1,0:T(8,128)(2,1)} %copy.724), channel_id=1, replica_groups=mesh['groups'=2,'tiles'=4,'chan'=2,'sub'=2] {'chan'}, dimensions={0}, use_global_device_ids=true | all-gather | bytes 104448 | tf_op jit(solution)/shard_map/all_gather | solution.py:167
  97.5 6.0 %collective-permute-start.4 = (bf16[8,64,68]{2,0,1:T(8,128)(2,1)}, bf16[8,64,68]{2,0,1:T(8,128)(2,1)}, u32[]{:S(2)}, u32[]{:S(2)}) collective-permute-start(bf16[8,64,68]{2,0,1:T(8,128)(2,1)} %copy.725), channel_id=1, source_target_pairs={{0,1},{1,4},{4,5},{5,8},{8,9},{9,12},{12,13},{2,3},{3,6},{6,7},{7,... | collective-permute-start | bytes 208904 | tf_op jit(solution)/shard_map/ppermute | solution.py:22
  103.5 1.9 fusion.27
  105.5 1.3 collective-permute-start.5
  106.7 1.5 copy.811
  109.4 2.2 collective-permute-done.5
  112.8 1.9 copy.732
  116.2 1.4 fusion.76
  117.6 1.6 copy.738
  119.2 1.6 copy.733
  120.7 1.0 copy.729
  122.4 1.0 copy.728
  123.4 1.7 pad_maximum_fusion.10
  125.2 1.7 copy.745
  129.2 1.5 maximum_maximum_fusion.2
  131.7 1.7 copy.748
  133.4 1.7 copy.747
  135.1 1.7 copy.746
  137.9 1.8 copy.743
  139.6 1.7 copy.742
  141.4 1.8 copy.741
  147.4 1.3 fusion.31
  151.7 1.5 concatenate.155
  154.0 5.1 %all_gather.23 = bf16[8,64,68]{2,1,0:T(8,128)(2,1)S(1)} all-gather(bf16[4,64,68]{2,1,0:T(8,128)(2,1)} %copy.757), channel_id=1, replica_groups=mesh['groups'=2,'tiles'=4,'chan'=2,'sub'=2] {'chan'}, dimensions={0}, use_global_device_ids=true | all-gather | bytes 104448 | tf_op jit(solution)/shard_map/all_gather | solution.py:167
  159.8 4.9 %collective-permute-start.6 = (bf16[8,64,68]{2,0,1:T(8,128)(2,1)}, bf16[8,64,68]{2,0,1:T(8,128)(2,1)}, u32[]{:S(2)}, u32[]{:S(2)}) collective-permute-start(bf16[8,64,68]{2,0,1:T(8,128)(2,1)} %copy.758), channel_id=1, source_target_pairs={{0,1},{1,4},{4,5},{5,8},{8,9},{9,12},{12,13},{2,3},{3,6},{6,7},{7,... | collective-permute-start | bytes 208904 | tf_op jit(solution)/shard_map/ppermute | solution.py:22
  164.9 2.0 fusion.25
  166.8 1.3 collective-permute-start.7
  168.1 1.5 copy.807
  172.8 1.9 copy.765
  176.2 1.4 fusion.74
  177.6 1.6 copy.771
  180.2 1.0 copy.762
  181.9 1.0 copy.761
  182.9 1.7 pad_maximum_fusion.8
  184.7 1.7 copy.778
  188.6 1.5 maximum_maximum_fusion.3
  191.1 1.7 copy.781
  192.9 1.7 copy.780
  194.6 1.7 copy.779
  197.3 1.8 copy.776
  199.1 1.7 copy.775
  200.8 1.8 copy.774
  213.6 1.2 copy.784
  214.8 3.5 %all-to-all-start.2 = ((bf16[4,256,256]{2,0,1:T(4,128)(2,1)}), bf16[4,256,256]{2,0,1:T(4,128)(2,1)S(1)}, u32[]{:S(2)}, u32[]{:S(2)}) async-start(bf16[4,256,256]{2,0,1:T(4,128)(2,1)} %copy.784), calls=%async_computation.2 | async-start | bytes 1048576 | tf_op jit(solution)/shard_map/all_to_all | solution.py:216
  220.6 12.8 %reduce-scatter.17.cloned.1.call-done = bf16[9,32,64]{2,0,1:T(8,128)(2,1)} async-done(((bf16[9,64,64]{2,0,1:T(8,128)(2,1)}), bf16[9,32,64]{2,0,1:T(8,128)(2,1)}) %reduce-scatter.17.cloned.1.call-update) | async-done | bytes 36880 | tf_op jit(solution)/shard_map/reduce_scatter | solution.py:210
  233.5 13.9 %reduce-scatter.15.cloned.1.call-done = bf16[9,32,64]{2,0,1:T(8,128)(2,1)} async-done(((bf16[9,64,64]{2,0,1:T(8,128)(2,1)}), bf16[9,32,64]{2,0,1:T(8,128)(2,1)}) %reduce-scatter.15.cloned.1.call-update) | async-done | bytes 36880 | tf_op jit(solution)/shard_map/reduce_scatter | solution.py:210
  247.4 1.9 maximum_convert_fusion
  249.2 58.5 %all-reduce.3.cloned.1.call-done = (f32[2,128,64]{1,2,0:T(8,128)}, f32[2,9,32,64]{3,1,2,0:T(8,128)}, f32[2,128,64]{1,2,0:T(8,128)}) async-done(((f32[2,128,64]{1,2,0:T(8,128)}, f32[2,9,32,64]{3,1,2,0:T(8,128)}, f32[2,128,64]{1,2,0:T(8,128)}), (f32[2,128,64]{1,2,0:T(8,128)}, f32[2,9,32,64]{3,1,2,0:T(8,128)}, f32[2,128,64]{1,2,0:T(8,128)})) %all-reduce.3.cloned.1.call-update) | async-done | bytes 278544 | tf_op jit(solution)/shard_map/psum | solution.py:243
  307.7 1.9 copy.788
  (298 shorter events, 74.1 us)
Async XLA Ops:
  7.2 16.7 %copy-start.36 = (bf16[2,128,64]{1,2,0:T(8,128)(2,1)S(1)}, bf16[2,128,64]{1,2,0:T(8,128)(2,1)}, u32[]{:S(2)}) copy-start(bf16[2,128,64]{1,2,0:T(8,128)(2,1)} %param.10) | copy-start | bytes 98308
  7.2 25.0 %copy-start.37 = (bf16[2,128,64]{1,2,0:T(8,128)(2,1)S(1)}, bf16[2,128,64]{1,2,0:T(8,128)(2,1)}, u32[]{:S(2)}) copy-start(bf16[2,128,64]{1,2,0:T(8,128)(2,1)} %param.12) | copy-start | bytes 98308
  7.2 13.1 %all-to-all-start.1 = ((bf16[8,128,256]{2,1,0:T(8,128)(2,1)}), bf16[8,128,256]{2,1,0:T(8,128)(2,1)S(1)}, u32[]{:S(2)}, u32[]{:S(2)}) async-start(bf16[8,128,256]{2,1,0:T(8,128)(2,1)} %param.8), calls=%async_computation.1 | async-start | bytes 1048576 | tf_op jit(solution)/shard_map/all_to_all | solution.py:151
  20.3 16.6 %all-to-all-start = ((bf16[8,128,256]{2,1,0:T(8,128)(2,1)}), bf16[8,128,256]{2,1,0:T(8,128)(2,1)S(1)}, u32[]{:S(2)}, u32[]{:S(2)}) async-start(bf16[8,128,256]{2,1,0:T(8,128)(2,1)} %param.9), calls=%async_computation | async-start | bytes 1048576 | tf_op jit(solution)/shard_map/all_to_all | solution.py:152
  23.8 184.8 %reduce-scatter.25.cloned.1.call-start = ((), (), s32[]{:S(2)}) async-start(), calls=%async_computation.14 | async-start | bytes 98304
  32.2 24.1 %copy-start.26 = (bf16[2,256,64]{1,2,0:T(8,128)(2,1)}, bf16[2,256,64]{1,2,0:T(8,128)(2,1)S(1)}, u32[]{:S(2)}) copy-start(bf16[2,256,64]{1,2,0:T(8,128)(2,1)S(1)} %all_gather.18) | copy-start | bytes 196612
  36.8 17.9 %copy-start.31 = (bf16[2,256,64]{1,2,0:T(8,128)(2,1)}, bf16[2,256,64]{1,2,0:T(8,128)(2,1)S(1)}, u32[]{:S(2)}) copy-start(bf16[2,256,64]{1,2,0:T(8,128)(2,1)S(1)} %all_gather.20) | copy-start | bytes 196612
  43.8 4.4 %collective-permute-start.1 = (bf16[8,64,68]{1,0,2:T(8,128)(2,1)S(1)}, bf16[8,64,68]{1,0,2:T(8,128)(2,1)S(1)}, u32[]{:S(2)}, u32[]{:S(2)}) collective-permute-start(bf16[8,64,68]{1,0,2:T(8,128)(2,1)S(1)} %copy.661), channel_id=1, source_target_pairs={{1,0},{4,1},{5,4},{8,5},{9,8},{12,9},{13,12},{3,2},{6,3},{7,6},{10... | collective-permute-start | bytes 208904 | tf_op jit(solution)/shard_map/ppermute | solution.py:24
  45.1 4.0 %collective-permute-start = (bf16[8,64,68]{1,0,2:T(8,128)(2,1)S(1)}, bf16[8,64,68]{1,0,2:T(8,128)(2,1)S(1)}, u32[]{:S(2)}, u32[]{:S(2)}) collective-permute-start(bf16[8,64,68]{1,0,2:T(8,128)(2,1)S(1)} %copy.661), channel_id=1, source_target_pairs={{0,1},{1,4},{4,5},{5,8},{8,9},{9,12},{12,13},{2,3},{3,6},{6,7},{7,... | collective-permute-start | bytes 208904 | tf_op jit(solution)/shard_map/ppermute | solution.py:22
  53.3 1.0 copy-start.6
  54.6 1.4 copy-start.23
  56.1 0.8 copy-start.4
  62.5 4.8 %collective-permute-start.3 = (bf16[8,64,68]{1,0,2:T(8,128)(2,1)S(1)}, bf16[8,64,68]{1,0,2:T(8,128)(2,1)S(1)}, u32[]{:S(2)}, u32[]{:S(2)}) collective-permute-start(bf16[8,64,68]{1,0,2:T(8,128)(2,1)S(1)} %copy.693), channel_id=1, source_target_pairs={{1,0},{4,1},{5,4},{8,5},{9,8},{12,9},{13,12},{3,2},{6,3},{7,6},{10... | collective-permute-start | bytes 208904 | tf_op jit(solution)/shard_map/ppermute | solution.py:24
  63.8 4.5 %collective-permute-start.2 = (bf16[8,64,68]{1,0,2:T(8,128)(2,1)S(1)}, bf16[8,64,68]{1,0,2:T(8,128)(2,1)S(1)}, u32[]{:S(2)}, u32[]{:S(2)}) collective-permute-start(bf16[8,64,68]{1,0,2:T(8,128)(2,1)S(1)} %copy.693), channel_id=1, source_target_pairs={{0,1},{1,4},{4,5},{5,8},{8,9},{9,12},{12,13},{2,3},{3,6},{6,7},{7,... | collective-permute-start | bytes 208904 | tf_op jit(solution)/shard_map/ppermute | solution.py:22
  80.3 5.7 %copy-start.16 = (bf16[1,4,64,256]{3,2,1,0:T(8,128)(2,1)S(1)}, bf16[1,4,64,256]{3,2,1,0:T(8,128)(2,1)}, u32[]{:S(2)}) copy-start(bf16[1,4,64,256]{3,2,1,0:T(8,128)(2,1)} %copy.716) | copy-start | bytes 393220
  84.0 2.3 copy-start.9
  84.0 2.3 copy-start.32
  87.0 0.8 copy-start.5
  88.0 35.4 %copy-start.1 = (bf16[4,64,256]{1,2,0:T(8,128)(2,1)}, bf16[4,64,256]{1,2,0:T(8,128)(2,1)S(1)}, u32[]{:S(2)}) copy-start(bf16[4,64,256]{1,2,0:T(8,128)(2,1)S(1)} %copy.718) | copy-start | bytes 393220
  97.5 10.8 %collective-permute-start.4 = (bf16[8,64,68]{2,0,1:T(8,128)(2,1)}, bf16[8,64,68]{2,0,1:T(8,128)(2,1)}, u32[]{:S(2)}, u32[]{:S(2)}) collective-permute-start(bf16[8,64,68]{2,0,1:T(8,128)(2,1)} %copy.725), channel_id=1, source_target_pairs={{0,1},{1,4},{4,5},{5,8},{8,9},{9,12},{12,13},{2,3},{3,6},{6,7},{7,... | collective-permute-start | bytes 208904 | tf_op jit(solution)/shard_map/ppermute | solution.py:22
  105.5 6.1 %collective-permute-start.5 = (bf16[8,64,68]{2,0,1:T(8,128)(2,1)}, bf16[8,64,68]{2,0,1:T(8,128)(2,1)S(1)}, u32[]{:S(2)}, u32[]{:S(2)}) collective-permute-start(bf16[8,64,68]{2,0,1:T(8,128)(2,1)} %copy.725), channel_id=1, source_target_pairs={{1,0},{4,1},{5,4},{8,5},{9,8},{12,9},{13,12},{3,2},{6,3},{7,6},{10... | collective-permute-start | bytes 208904 | tf_op jit(solution)/shard_map/ppermute | solution.py:24
  108.3 102.6 %reduce-scatter.23.cloned.1.call-start = ((), (), s32[]{:S(2)}) async-start(), calls=%async_computation.13 | async-start | bytes 98304
  123.4 1.8 copy-start.29
  137.8 8.1 %copy-start.14 = (bf16[1,4,64,256]{3,2,1,0:T(8,128)(2,1)S(1)}, bf16[1,4,64,256]{3,2,1,0:T(8,128)(2,1)}, u32[]{:S(2)}) copy-start(bf16[1,4,64,256]{3,2,1,0:T(8,128)(2,1)} %copy.744) | copy-start | bytes 393220
  137.8 8.1 %copy-start.12 = (bf16[1,4,64,256]{3,2,1,0:T(8,128)(2,1)S(1)}, bf16[1,4,64,256]{3,2,1,0:T(8,128)(2,1)}, u32[]{:S(2)}) copy-start(bf16[1,4,64,256]{3,2,1,0:T(8,128)(2,1)} %copy.745) | copy-start | bytes 393220
  141.4 4.7 %copy-start.19 = (bf16[1,4,64,256]{3,2,1,0:T(8,128)(2,1)S(1)}, bf16[1,4,64,256]{3,2,1,0:T(8,128)(2,1)}, u32[]{:S(2)}) copy-start(bf16[1,4,64,256]{3,2,1,0:T(8,128)(2,1)} %copy.747) | copy-start | bytes 393220
  141.4 4.8 %copy-start.17 = (bf16[1,4,64,256]{3,2,1,0:T(8,128)(2,1)S(1)}, bf16[1,4,64,256]{3,2,1,0:T(8,128)(2,1)}, u32[]{:S(2)}) copy-start(bf16[1,4,64,256]{3,2,1,0:T(8,128)(2,1)} %copy.748) | copy-start | bytes 393220
  143.1 2.9 copy-start.21
  143.1 3.0 copy-start.7
  146.0 1.0 copy-start.10
  146.0 1.0 copy-start.27
  146.0 1.4 copy-start.38
  146.5 2.3 copy-start.25
  147.4 1.4 copy-start.24
  147.4 1.6 copy-start.33
  149.5 20.1 %copy-start.2 = (bf16[4,64,256]{2,1,0:T(8,128)(2,1)}, bf16[4,64,256]{2,1,0:T(8,128)(2,1)S(1)}, u32[]{:S(2)}) copy-start(bf16[4,64,256]{2,1,0:T(8,128)(2,1)S(1)} %add_convert_fusion.1) | copy-start | bytes 393220
  149.7 33.2 %copy-start = (bf16[4,64,256]{1,2,0:T(8,128)(2,1)}, bf16[4,64,256]{1,2,0:T(8,128)(2,1)S(1)}, u32[]{:S(2)}) copy-start(bf16[4,64,256]{1,2,0:T(8,128)(2,1)S(1)} %copy.751) | copy-start | bytes 393220
  159.8 9.8 %collective-permute-start.6 = (bf16[8,64,68]{2,0,1:T(8,128)(2,1)}, bf16[8,64,68]{2,0,1:T(8,128)(2,1)}, u32[]{:S(2)}, u32[]{:S(2)}) collective-permute-start(bf16[8,64,68]{2,0,1:T(8,128)(2,1)} %copy.758), channel_id=1, source_target_pairs={{0,1},{1,4},{4,5},{5,8},{8,9},{9,12},{12,13},{2,3},{3,6},{6,7},{7,... | collective-permute-start | bytes 208904 | tf_op jit(solution)/shard_map/ppermute | solution.py:22
  164.8 47.6 %reduce-scatter.21.cloned.1.call-start = ((), (), s32[]{:S(2)}) async-start(), calls=%async_computation.12 | async-start | bytes 98304
  166.8 3.9 %collective-permute-start.7 = (bf16[8,64,68]{2,0,1:T(8,128)(2,1)}, bf16[8,64,68]{2,0,1:T(8,128)(2,1)}, u32[]{:S(2)}, u32[]{:S(2)}) collective-permute-start(bf16[8,64,68]{2,0,1:T(8,128)(2,1)} %copy.758), channel_id=1, source_target_pairs={{1,0},{4,1},{5,4},{8,5},{9,8},{12,9},{13,12},{3,2},{6,3},{7,6},{10... | collective-permute-start | bytes 208904 | tf_op jit(solution)/shard_map/ppermute | solution.py:24
  169.6 49.5 %reduce-scatter.19.cloned.1.call-start = ((), (), s32[]{:S(2)}) async-start(), calls=%async_computation.11 | async-start | bytes 98304
  182.9 1.7 copy-start.30
  197.3 8.1 %copy-start.15 = (bf16[1,4,64,256]{3,2,1,0:T(8,128)(2,1)S(1)}, bf16[1,4,64,256]{3,2,1,0:T(8,128)(2,1)}, u32[]{:S(2)}) copy-start(bf16[1,4,64,256]{3,2,1,0:T(8,128)(2,1)} %copy.777) | copy-start | bytes 393220
  197.3 8.1 %copy-start.3 = (bf16[4,64,256]{2,1,0:T(8,128)(2,1)S(1)}, bf16[4,64,256]{2,1,0:T(8,128)(2,1)}, u32[]{:S(2)}) copy-start(bf16[4,64,256]{2,1,0:T(8,128)(2,1)} %copy-done.2) | copy-start | bytes 393220
  197.3 8.2 %copy-start.13 = (bf16[1,4,64,256]{3,2,1,0:T(8,128)(2,1)S(1)}, bf16[1,4,64,256]{3,2,1,0:T(8,128)(2,1)}, u32[]{:S(2)}) copy-start(bf16[1,4,64,256]{3,2,1,0:T(8,128)(2,1)} %copy.778) | copy-start | bytes 393220
  200.8 4.7 %copy-start.18 = (bf16[1,4,64,256]{3,2,1,0:T(8,128)(2,1)S(1)}, bf16[1,4,64,256]{3,2,1,0:T(8,128)(2,1)}, u32[]{:S(2)}) copy-start(bf16[1,4,64,256]{3,2,1,0:T(8,128)(2,1)} %copy.781) | copy-start | bytes 393220
  202.6 2.9 copy-start.22
  202.6 2.9 copy-start.20
  202.6 3.0 copy-start.8
  207.0 26.5 %reduce-scatter.17.cloned.1.call-start = ((), (), s32[]{:S(2)}) async-start(), calls=%async_computation.10 | async-start | bytes 393216 | tf_op jit(solution)/shard_map/reduce_scatter | solution.py:210
  208.5 38.9 %reduce-scatter.15.cloned.1.call-start = ((), (), s32[]{:S(2)}) async-start(), calls=%async_computation.9 | async-start | bytes 393216 | tf_op jit(solution)/shard_map/reduce_scatter | solution.py:210
  209.4 3.8 %copy-start.11 = (bf16[4,256,256]{2,1,0:T(8,128)(2,1)S(1)}, bf16[4,256,256]{2,1,0:T(8,128)(2,1)}, u32[]{:S(2)}) copy-start(bf16[4,256,256]{2,1,0:T(8,128)(2,1)} %get-tuple-element.146) | copy-start | bytes 1572868
  209.4 3.8 %copy-start.28 = (bf16[2,256,64]{1,2,0:T(8,128)(2,1)S(1)}, bf16[2,256,64]{1,2,0:T(8,128)(2,1)}, u32[]{:S(2)}) copy-start(bf16[2,256,64]{1,2,0:T(8,128)(2,1)} %copy-done.26) | copy-start | bytes 196612
  214.8 94.8 %all-to-all-start.2 = ((bf16[4,256,256]{2,0,1:T(4,128)(2,1)}), bf16[4,256,256]{2,0,1:T(4,128)(2,1)S(1)}, u32[]{:S(2)}, u32[]{:S(2)}) async-start(bf16[4,256,256]{2,0,1:T(4,128)(2,1)} %copy.784), calls=%async_computation.2 | async-start | bytes 1048576 | tf_op jit(solution)/shard_map/all_to_all | solution.py:216
  218.3 89.4 %all-reduce.3.cloned.1.call-start = ((), (), s32[]{:S(2)}) async-start(), calls=%async_computation.15 | async-start | bytes 1310720 | tf_op jit(solution)/shard_map/psum | solution.py:243
  307.7 2.8 copy-start.35
  307.7 3.4 %copy-start.34 = (f32[2,128,64]{1,2,0:T(8,128)S(1)}, f32[2,128,64]{1,2,0:T(8,128)}, u32[]{:S(2)}) copy-start(f32[2,128,64]{1,2,0:T(8,128)} %get-tuple-element.152) | copy-start | bytes 196612
Sparse Core Ops, SparseCore 0:
  108.4 13.9 reduce-scatter.24
  164.9 9.3 reduce-scatter.22
  177.1 9.8 reduce-scatter.20
  207.1 11.9 reduce-scatter.18
  221.8 11.6 reduce-scatter.16
  235.6 11.6 reduce-scatter.14
  250.5 57.1 all-reduce.2
where the time goes:
time: 321 us; the launch traced here: 319 us
  local copies, waits for them, and re-layouts  106 us (33%)
  waiting for transfers between devices  96.8 us (30%)
  starting transfers between devices  34.3 us (11%)
  blocking collectives  33.1 us (10%)
  other arithmetic  16.8 us (5%)
  between operations  16.2 us (5%)
  matrix products  15 us (5%)
    psum x1, waiting for transfers between devices, local(): lax.psum((down_gradient, core_gradient, up_gradient), ('tiles', 'sub'))  58.5 us
    unnamed x132, local copies, waits for them, and re-layouts  27.1 us
    reduce_scatter x2, waiting for transfers between devices, whole_tiles(): lax.psum_scatter(core_part.astype(jnp.bfloat16), 'chan', scatter_dimensio...  26.7 us
    another operation x18, local copies, waits for them, and re-layouts, stacked_windows(): jnp.stack([window(padded, 2 - offset // 3, 2 - offset % 3) for offset in...  25.9 us
    all_gather x4, blocking collectives, padded_of(): owner_cycle = lax.all_gather(border, 'chan', axis=0, tiled=True)  20.2 us
    ppermute x4, starting transfers between devices, padded_2(): lax.ppermute(tail, axis, [(i, (i + 1) % count) for i in range(ends)])  17.6 us
    slice x20, local copies, waits for them, and re-layouts, place_border(): nearest[:, which_side, :, piece_index * TILE:(piece_index + 1) * TILE]  14.6 us
    another operation x18, local copies, waits for them, and re-layouts, stacked_windows(): jnp.stack([window(padded, offset // 3, offset % 3) for offset in range(9)...  8.53 us
  transfers between devices with their start and end apart: 18, of which 8 were waited for; matrix products, arithmetic and copies ran while one was open for 32% of the time, Pallas kernels for 0%

commit v1 on v0

--- a/solution.py
+++ b/solution.py
@@ -241,7 +241,7 @@
     core_gradient = jnp.stack(core_list, axis=0)
     up_gradient = jnp.stack(up_list, axis=0)
     down_gradient, core_gradient, up_gradient = lax.psum(
-        (down_gradient, core_gradient, up_gradient), ("tiles", "sub")
+        lax.psum((down_gradient, core_gradient, up_gradient), "sub"), "tiles"
     )
     return (upstream, down_gradient, core_gradient, up_gradient)
 

time: 321 us -> 329 us (1.025)
  blocking collectives: 33.1 us -> 44.3 us
  starting transfers between devices: 34.3 us -> 30.9 us
    all_to_all x0 -> x1, blocking collectives: none -> 11.2 us  [whole_tiles(): lax.all_to_all(upstream, 'chan', split_axis=1, concat_axis=0, tiled=True)]
    psum x1 -> x2, waiting for transfers between devices: 58.5 us -> 52.4 us  [the longest x1 32.2 us: local(): lax.psum(lax.psum((down_gradient, core_gradient, up_gradient), 'sub'), 't...]
    unnamed x11 -> x12, waiting for transfers between devices: 0.97 us -> 6.01 us
    all_to_all x1 -> x0, starting transfers between devices: 3.49 us -> none  [whole_tiles(): lax.all_to_all(upstream, 'chan', split_axis=1, concat_axis=0, tiled=True)]
    unnamed x132 -> x128, local copies, waits for them, and re-layouts: 27.1 us -> 28.8 us
  transfers between devices with their start and end apart: 18 -> 18, of which waited for: 8 -> 9; matrix products, arithmetic and copies ran while one was open for 32% -> 30% of each run, Pallas kernels for 0% -> 0%
where the time goes in v1:
time: 329 us; the launch traced here: 326 us
  local copies, waits for them, and re-layouts  107 us (33%)
  waiting for transfers between devices  95.8 us (29%)
  blocking collectives  44.3 us (13%)
  starting transfers between devices  30.9 us (9%)
  other arithmetic  16.8 us (5%)
  between operations  16.2 us (5%)
  matrix products  15 us (5%)
    psum x1, waiting for transfers between devices, local(): lax.psum(lax.psum((down_gradient, core_gradient, up_gradient), 'sub'), 't...  32.2 us
    unnamed x128, local copies, waits for them, and re-layouts  28.8 us
    reduce_scatter x2, waiting for transfers between devices, whole_tiles(): lax.psum_scatter(core_part.astype(jnp.bfloat16), 'chan', scatter_dimensio...  26.7 us
    another operation x18, local copies, waits for them, and re-layouts, stacked_windows(): jnp.stack([window(padded, 2 - offset // 3, 2 - offset % 3) for offset in...  25.9 us
    psum x1, waiting for transfers between devices, local(): lax.psum((down_gradient, core_gradient, up_gradient), 'sub')  20.3 us
    all_gather x4, blocking collectives, padded_of(): owner_cycle = lax.all_gather(border, 'chan', axis=0, tiled=True)  20.2 us
    ppermute x4, starting transfers between devices, padded_2(): lax.ppermute(tail, axis, [(i, (i + 1) % count) for i in range(ends)])  17.6 us
    slice x20, local copies, waits for them, and re-layouts, place_border(): nearest[:, which_side, :, piece_index * TILE:(piece_index + 1) * TILE]  14.6 us
  transfers between devices with their start and end apart: 18, of which 9 were waited for; matrix products, arithmetic and copies ran while one was open for 30% of the time, Pallas kernels for 0%

profile of v1, /device:TPU:0, one launch (start us, length us, event | category | flops | bytes accessed | tf_op | source)
XLA Modules:
  0.0 326.3 jit_solution(10704132441250115852)
XLA Ops:
  7.2 4.3 %all-to-all-start.1 = ((bf16[8,128,256]{2,1,0:T(8,128)(2,1)}), bf16[8,128,256]{2,1,0:T(8,128)(2,1)S(1)}, u32[]{:S(2)}, u32[]{:S(2)}) async-start(bf16[8,128,256]{2,1,0:T(8,128)(2,1)} %param.8), calls=%async_computation.1 | async-start | bytes 1048576 | tf_op jit(solution)/shard_map/all_to_all | solution.py:151
  13.7 6.6 %all-to-all-done.1 = bf16[8,128,256]{2,1,0:T(8,128)(2,1)S(1)} async-done(((bf16[8,128,256]{2,1,0:T(8,128)(2,1)}), bf16[8,128,256]{2,1,0:T(8,128)(2,1)S(1)}, u32[]{:S(2)}, u32[]{:S(2)}) %all-to-all-start.1) | async-done | bytes 524320 | tf_op jit(solution)/shard_map/all_to_all | solution.py:151
  20.3 3.5 %all-to-all-start = ((bf16[8,128,256]{2,1,0:T(8,128)(2,1)}), bf16[8,128,256]{2,1,0:T(8,128)(2,1)S(1)}, u32[]{:S(2)}, u32[]{:S(2)}) async-start(bf16[8,128,256]{2,1,0:T(8,128)(2,1)} %param.9), calls=%async_computation | async-start | bytes 1048576 | tf_op jit(solution)/shard_map/all_to_all | solution.py:152
  23.8 8.3 %all_gather.18 = bf16[2,256,64]{1,2,0:T(8,128)(2,1)S(1)} all-gather(bf16[2,128,64]{1,2,0:T(8,128)(2,1)S(1)} %copy-done.34), channel_id=1, replica_groups=mesh['groups'=2,'tiles'=4,'chan'=2,'sub'=2] {'chan'}, dimensions={1}, use_global_device_ids=true | all-gather | bytes 98304 | tf_op jit(solution)/shard_map/all_gather | solution.py:158
  32.2 4.6 %all_gather.20 = bf16[2,256,64]{1,2,0:T(8,128)(2,1)S(1)} all-gather(bf16[2,128,64]{1,2,0:T(8,128)(2,1)S(1)} %copy-done.35), channel_id=1, replica_groups=mesh['groups'=2,'tiles'=4,'chan'=2,'sub'=2] {'chan'}, dimensions={1}, use_global_device_ids=true | all-gather | bytes 98304 | tf_op jit(solution)/shard_map/all_gather | solution.py:159
  38.7 4.9 %all_gather.19 = bf16[8,64,68]{2,1,0:T(8,128)(2,1)S(1)} all-gather(bf16[4,64,68]{2,1,0:T(8,128)(2,1)S(1)} %copy.660), channel_id=1, replica_groups=mesh['groups'=2,'tiles'=4,'chan'=2,'sub'=2] {'chan'}, dimensions={0}, use_global_device_ids=true | all-gather | bytes 104448 | tf_op jit(solution)/shard_map/all_gather | solution.py:167
  43.8 1.3 collective-permute-start.1
  45.1 3.0 collective-permute-start
  54.6 1.4 add_convert_fusion
  57.4 4.9 %all_gather.21 = bf16[8,64,68]{2,1,0:T(8,128)(2,1)S(1)} all-gather(bf16[4,64,68]{2,1,0:T(8,128)(2,1)S(1)} %copy.692), channel_id=1, replica_groups=mesh['groups'=2,'tiles'=4,'chan'=2,'sub'=2] {'chan'}, dimensions={0}, use_global_device_ids=true | all-gather | bytes 104448 | tf_op jit(solution)/shard_map/all_gather | solution.py:167
  62.5 1.3 collective-permute-start.3
  63.8 3.5 %collective-permute-start.2 = (bf16[8,64,68]{1,0,2:T(8,128)(2,1)S(1)}, bf16[8,64,68]{1,0,2:T(8,128)(2,1)S(1)}, u32[]{:S(2)}, u32[]{:S(2)}) collective-permute-start(bf16[8,64,68]{1,0,2:T(8,128)(2,1)S(1)} %copy.693), channel_id=1, source_target_pairs={{0,1},{1,4},{4,5},{5,8},{8,9},{9,12},{12,13},{2,3},{3,6},{6,7},{7,... | collective-permute-start | bytes 208904 | tf_op jit(solution)/shard_map/ppermute | solution.py:22
  72.8 1.7 copy.716
  77.0 1.7 copy.711
  89.4 1.5 concatenate.146
  91.6 5.1 %all_gather.22 = bf16[8,64,68]{2,1,0:T(8,128)(2,1)S(1)} all-gather(bf16[4,64,68]{2,1,0:T(8,128)(2,1)} %copy.724), channel_id=1, replica_groups=mesh['groups'=2,'tiles'=4,'chan'=2,'sub'=2] {'chan'}, dimensions={0}, use_global_device_ids=true | all-gather | bytes 104448 | tf_op jit(solution)/shard_map/all_gather | solution.py:167
  97.5 6.0 %collective-permute-start.4 = (bf16[8,64,68]{2,0,1:T(8,128)(2,1)}, bf16[8,64,68]{2,0,1:T(8,128)(2,1)}, u32[]{:S(2)}, u32[]{:S(2)}) collective-permute-start(bf16[8,64,68]{2,0,1:T(8,128)(2,1)} %copy.725), channel_id=1, source_target_pairs={{0,1},{1,4},{4,5},{5,8},{8,9},{9,12},{12,13},{2,3},{3,6},{6,7},{7,... | collective-permute-start | bytes 208904 | tf_op jit(solution)/shard_map/ppermute | solution.py:22
  103.5 1.9 fusion.27
  105.5 1.3 collective-permute-start.5
  106.8 1.5 copy.811
  109.4 2.2 collective-permute-done.5
  112.8 1.9 copy.732
  116.1 1.4 fusion.76
  117.5 1.6 copy.738
  119.1 1.6 copy.733
  123.4 1.7 pad_maximum_fusion.10
  125.2 1.7 copy.745
  129.1 1.5 maximum_maximum_fusion.2
  131.7 1.7 copy.748
  133.4 1.7 copy.747
  135.1 1.7 copy.746
  137.8 1.8 copy.743
  139.6 1.7 copy.742
  141.3 1.8 copy.741
  147.4 1.3 fusion.31
  151.7 1.5 concatenate.155
  153.9 5.1 %all_gather.23 = bf16[8,64,68]{2,1,0:T(8,128)(2,1)S(1)} all-gather(bf16[4,64,68]{2,1,0:T(8,128)(2,1)} %copy.757), channel_id=1, replica_groups=mesh['groups'=2,'tiles'=4,'chan'=2,'sub'=2] {'chan'}, dimensions={0}, use_global_device_ids=true | all-gather | bytes 104448 | tf_op jit(solution)/shard_map/all_gather | solution.py:167
  159.8 4.9 %collective-permute-start.6 = (bf16[8,64,68]{2,0,1:T(8,128)(2,1)}, bf16[8,64,68]{2,0,1:T(8,128)(2,1)}, u32[]{:S(2)}, u32[]{:S(2)}) collective-permute-start(bf16[8,64,68]{2,0,1:T(8,128)(2,1)} %copy.758), channel_id=1, source_target_pairs={{0,1},{1,4},{4,5},{5,8},{8,9},{9,12},{12,13},{2,3},{3,6},{6,7},{7,... | collective-permute-start | bytes 208904 | tf_op jit(solution)/shard_map/ppermute | solution.py:22
  164.8 2.0 fusion.25
  166.8 1.3 collective-permute-start.7
  168.1 1.5 copy.807
  172.8 1.9 copy.765
  176.2 1.4 fusion.74
  177.6 1.6 copy.771
  180.2 1.0 copy.762
  182.9 1.7 pad_maximum_fusion.8
  184.7 1.7 copy.778
  188.6 1.5 maximum_maximum_fusion.3
  191.1 1.7 copy.781
  192.9 1.7 copy.780
  194.6 1.7 copy.779
  197.3 1.8 copy.776
  199.1 1.7 copy.775
  200.8 1.8 copy.774
  213.3 5.8 %reduce-scatter.19.cloned.1.call-done = bf16[128,64]{1,0:T(8,128)(2,1)} async-done(((bf16[256,64]{1,0:T(8,128)(2,1)}), bf16[128,64]{1,0:T(8,128)(2,1)}) %reduce-scatter.19.cloned.1.call-update) | async-done | bytes 16400
  220.7 12.8 %reduce-scatter.17.cloned.1.call-done = bf16[9,32,64]{2,0,1:T(8,128)(2,1)} async-done(((bf16[9,64,64]{2,0,1:T(8,128)(2,1)}), bf16[9,32,64]{2,0,1:T(8,128)(2,1)}) %reduce-scatter.17.cloned.1.call-update) | async-done | bytes 36880 | tf_op jit(solution)/shard_map/reduce_scatter | solution.py:210
  233.5 13.9 %reduce-scatter.15.cloned.1.call-done = bf16[9,32,64]{2,0,1:T(8,128)(2,1)} async-done(((bf16[9,64,64]{2,0,1:T(8,128)(2,1)}), bf16[9,32,64]{2,0,1:T(8,128)(2,1)}) %reduce-scatter.15.cloned.1.call-update) | async-done | bytes 36880 | tf_op jit(solution)/shard_map/reduce_scatter | solution.py:210
  247.4 1.8 maximum_convert_fusion
  249.3 20.3 %all-reduce.7.cloned.1.call-done = (f32[2,128,64]{1,2,0:T(8,128)}, f32[2,9,32,64]{3,1,2,0:T(8,128)}, f32[2,128,64]{1,2,0:T(8,128)}) async-done(((f32[2,128,64]{1,2,0:T(8,128)}, f32[2,9,32,64]{3,1,2,0:T(8,128)}, f32[2,128,64]{1,2,0:T(8,128)}), (f32[2,128,64]{1,2,0:T(8,128)}, f32[2,9,32,64]{3,1,2,0:T(8,128)}, f32[2,128,64]{1,2,0:T(8,128)})) %all-reduce.7.cloned.1.call-update) | async-done | bytes 278544 | tf_op jit(solution)/shard_map/psum | solution.py:244
  270.4 11.2 %all_to_all.54 = bf16[4,256,256]{2,0,1:T(4,128)(2,1)S(1)} all-to-all(bf16[4,256,256]{2,0,1:T(4,128)(2,1)S(1)} %copy.784), channel_id=1, replica_groups=mesh['groups'=2,'tiles'=4,'chan'=2,'sub'=2] {'chan'}, dimensions={1} | all-to-all | bytes 1048576 | tf_op jit(solution)/shard_map/all_to_all | solution.py:216
  282.5 32.2 %all-reduce.5.cloned.1.call-done = (f32[2,128,64]{1,2,0:T(8,128)}, f32[2,9,32,64]{3,1,2,0:T(8,128)}, f32[2,128,64]{1,2,0:T(8,128)}) async-done(((f32[2,128,64]{1,2,0:T(8,128)}, f32[2,9,32,64]{3,1,2,0:T(8,128)}, f32[2,128,64]{1,2,0:T(8,128)}), (f32[2,128,64]{1,2,0:T(8,128)}, f32[2,9,32,64]{3,1,2,0:T(8,128)}, f32[2,128,64]{1,2,0:T(8,128)})) %all-reduce.5.cloned.1.call-update) | async-done | bytes 278544 | tf_op jit(solution)/shard_map/psum | solution.py:243
  314.6 1.8 copy.788
  316.5 1.5 copy.884
  318.0 1.5 copy.885
  (296 shorter events, 75.6 us)
Async XLA Ops:
  7.2 16.7 %copy-start.34 = (bf16[2,128,64]{1,2,0:T(8,128)(2,1)S(1)}, bf16[2,128,64]{1,2,0:T(8,128)(2,1)}, u32[]{:S(2)}) copy-start(bf16[2,128,64]{1,2,0:T(8,128)(2,1)} %param.10) | copy-start | bytes 98308
  7.2 25.0 %copy-start.35 = (bf16[2,128,64]{1,2,0:T(8,128)(2,1)S(1)}, bf16[2,128,64]{1,2,0:T(8,128)(2,1)}, u32[]{:S(2)}) copy-start(bf16[2,128,64]{1,2,0:T(8,128)(2,1)} %param.12) | copy-start | bytes 98308
  7.2 13.1 %all-to-all-start.1 = ((bf16[8,128,256]{2,1,0:T(8,128)(2,1)}), bf16[8,128,256]{2,1,0:T(8,128)(2,1)S(1)}, u32[]{:S(2)}, u32[]{:S(2)}) async-start(bf16[8,128,256]{2,1,0:T(8,128)(2,1)} %param.8), calls=%async_computation.1 | async-start | bytes 1048576 | tf_op jit(solution)/shard_map/all_to_all | solution.py:151
  20.3 16.6 %all-to-all-start = ((bf16[8,128,256]{2,1,0:T(8,128)(2,1)}), bf16[8,128,256]{2,1,0:T(8,128)(2,1)S(1)}, u32[]{:S(2)}, u32[]{:S(2)}) async-start(bf16[8,128,256]{2,1,0:T(8,128)(2,1)} %param.9), calls=%async_computation | async-start | bytes 1048576 | tf_op jit(solution)/shard_map/all_to_all | solution.py:152
  23.8 184.8 %reduce-scatter.25.cloned.1.call-start = ((), (), s32[]{:S(2)}) async-start(), calls=%async_computation.14 | async-start | bytes 98304
  32.2 24.1 %copy-start.26 = (bf16[2,256,64]{1,2,0:T(8,128)(2,1)}, bf16[2,256,64]{1,2,0:T(8,128)(2,1)S(1)}, u32[]{:S(2)}) copy-start(bf16[2,256,64]{1,2,0:T(8,128)(2,1)S(1)} %all_gather.18) | copy-start | bytes 196612
  36.8 17.9 %copy-start.31 = (bf16[2,256,64]{1,2,0:T(8,128)(2,1)}, bf16[2,256,64]{1,2,0:T(8,128)(2,1)S(1)}, u32[]{:S(2)}) copy-start(bf16[2,256,64]{1,2,0:T(8,128)(2,1)S(1)} %all_gather.20) | copy-start | bytes 196612
  43.8 4.4 %collective-permute-start.1 = (bf16[8,64,68]{1,0,2:T(8,128)(2,1)S(1)}, bf16[8,64,68]{1,0,2:T(8,128)(2,1)S(1)}, u32[]{:S(2)}, u32[]{:S(2)}) collective-permute-start(bf16[8,64,68]{1,0,2:T(8,128)(2,1)S(1)} %copy.661), channel_id=1, source_target_pairs={{1,0},{4,1},{5,4},{8,5},{9,8},{12,9},{13,12},{3,2},{6,3},{7,6},{10... | collective-permute-start | bytes 208904 | tf_op jit(solution)/shard_map/ppermute | solution.py:24
  45.1 4.0 %collective-permute-start = (bf16[8,64,68]{1,0,2:T(8,128)(2,1)S(1)}, bf16[8,64,68]{1,0,2:T(8,128)(2,1)S(1)}, u32[]{:S(2)}, u32[]{:S(2)}) collective-permute-start(bf16[8,64,68]{1,0,2:T(8,128)(2,1)S(1)} %copy.661), channel_id=1, source_target_pairs={{0,1},{1,4},{4,5},{5,8},{8,9},{9,12},{12,13},{2,3},{3,6},{6,7},{7,... | collective-permute-start | bytes 208904 | tf_op jit(solution)/shard_map/ppermute | solution.py:22
  53.3 1.0 copy-start.6
  54.6 1.4 copy-start.23
  56.1 0.8 copy-start.4
  62.5 4.8 %collective-permute-start.3 = (bf16[8,64,68]{1,0,2:T(8,128)(2,1)S(1)}, bf16[8,64,68]{1,0,2:T(8,128)(2,1)S(1)}, u32[]{:S(2)}, u32[]{:S(2)}) collective-permute-start(bf16[8,64,68]{1,0,2:T(8,128)(2,1)S(1)} %copy.693), channel_id=1, source_target_pairs={{1,0},{4,1},{5,4},{8,5},{9,8},{12,9},{13,12},{3,2},{6,3},{7,6},{10... | collective-permute-start | bytes 208904 | tf_op jit(solution)/shard_map/ppermute | solution.py:24
  63.8 4.5 %collective-permute-start.2 = (bf16[8,64,68]{1,0,2:T(8,128)(2,1)S(1)}, bf16[8,64,68]{1,0,2:T(8,128)(2,1)S(1)}, u32[]{:S(2)}, u32[]{:S(2)}) collective-permute-start(bf16[8,64,68]{1,0,2:T(8,128)(2,1)S(1)} %copy.693), channel_id=1, source_target_pairs={{0,1},{1,4},{4,5},{5,8},{8,9},{9,12},{12,13},{2,3},{3,6},{6,7},{7,... | collective-permute-start | bytes 208904 | tf_op jit(solution)/shard_map/ppermute | solution.py:22
  80.3 5.7 %copy-start.16 = (bf16[1,4,64,256]{3,2,1,0:T(8,128)(2,1)S(1)}, bf16[1,4,64,256]{3,2,1,0:T(8,128)(2,1)}, u32[]{:S(2)}) copy-start(bf16[1,4,64,256]{3,2,1,0:T(8,128)(2,1)} %copy.716) | copy-start | bytes 393220
  84.0 2.3 copy-start.9
  84.0 2.3 copy-start.32
  87.0 0.8 copy-start.5
  88.0 35.4 %copy-start.1 = (bf16[4,64,256]{1,2,0:T(8,128)(2,1)}, bf16[4,64,256]{1,2,0:T(8,128)(2,1)S(1)}, u32[]{:S(2)}) copy-start(bf16[4,64,256]{1,2,0:T(8,128)(2,1)S(1)} %copy.718) | copy-start | bytes 393220
  97.5 10.8 %collective-permute-start.4 = (bf16[8,64,68]{2,0,1:T(8,128)(2,1)}, bf16[8,64,68]{2,0,1:T(8,128)(2,1)}, u32[]{:S(2)}, u32[]{:S(2)}) collective-permute-start(bf16[8,64,68]{2,0,1:T(8,128)(2,1)} %copy.725), channel_id=1, source_target_pairs={{0,1},{1,4},{4,5},{5,8},{8,9},{9,12},{12,13},{2,3},{3,6},{6,7},{7,... | collective-permute-start | bytes 208904 | tf_op jit(solution)/shard_map/ppermute | solution.py:22
  105.5 6.1 %collective-permute-start.5 = (bf16[8,64,68]{2,0,1:T(8,128)(2,1)}, bf16[8,64,68]{2,0,1:T(8,128)(2,1)S(1)}, u32[]{:S(2)}, u32[]{:S(2)}) collective-permute-start(bf16[8,64,68]{2,0,1:T(8,128)(2,1)} %copy.725), channel_id=1, source_target_pairs={{1,0},{4,1},{5,4},{8,5},{9,8},{12,9},{13,12},{3,2},{6,3},{7,6},{10... | collective-permute-start | bytes 208904 | tf_op jit(solution)/shard_map/ppermute | solution.py:24
  108.3 102.7 %reduce-scatter.23.cloned.1.call-start = ((), (), s32[]{:S(2)}) async-start(), calls=%async_computation.13 | async-start | bytes 98304
  123.4 1.8 copy-start.29
  137.8 8.1 %copy-start.14 = (bf16[1,4,64,256]{3,2,1,0:T(8,128)(2,1)S(1)}, bf16[1,4,64,256]{3,2,1,0:T(8,128)(2,1)}, u32[]{:S(2)}) copy-start(bf16[1,4,64,256]{3,2,1,0:T(8,128)(2,1)} %copy.744) | copy-start | bytes 393220
  137.8 8.1 %copy-start.12 = (bf16[1,4,64,256]{3,2,1,0:T(8,128)(2,1)S(1)}, bf16[1,4,64,256]{3,2,1,0:T(8,128)(2,1)}, u32[]{:S(2)}) copy-start(bf16[1,4,64,256]{3,2,1,0:T(8,128)(2,1)} %copy.745) | copy-start | bytes 393220
  141.3 4.7 %copy-start.19 = (bf16[1,4,64,256]{3,2,1,0:T(8,128)(2,1)S(1)}, bf16[1,4,64,256]{3,2,1,0:T(8,128)(2,1)}, u32[]{:S(2)}) copy-start(bf16[1,4,64,256]{3,2,1,0:T(8,128)(2,1)} %copy.747) | copy-start | bytes 393220
  141.3 4.8 %copy-start.17 = (bf16[1,4,64,256]{3,2,1,0:T(8,128)(2,1)S(1)}, bf16[1,4,64,256]{3,2,1,0:T(8,128)(2,1)}, u32[]{:S(2)}) copy-start(bf16[1,4,64,256]{3,2,1,0:T(8,128)(2,1)} %copy.748) | copy-start | bytes 393220
  143.1 2.9 copy-start.21
  143.1 3.0 copy-start.7
  146.0 1.0 copy-start.10
  146.0 1.0 copy-start.27
  146.0 1.4 copy-start.36
  146.5 2.3 copy-start.25
  147.4 1.4 copy-start.24
  147.4 1.6 copy-start.33
  149.5 20.1 %copy-start.2 = (bf16[4,64,256]{2,1,0:T(8,128)(2,1)}, bf16[4,64,256]{2,1,0:T(8,128)(2,1)S(1)}, u32[]{:S(2)}) copy-start(bf16[4,64,256]{2,1,0:T(8,128)(2,1)S(1)} %add_convert_fusion.1) | copy-start | bytes 393220
  149.7 33.3 %copy-start = (bf16[4,64,256]{1,2,0:T(8,128)(2,1)}, bf16[4,64,256]{1,2,0:T(8,128)(2,1)S(1)}, u32[]{:S(2)}) copy-start(bf16[4,64,256]{1,2,0:T(8,128)(2,1)S(1)} %copy.751) | copy-start | bytes 393220
  159.8 9.8 %collective-permute-start.6 = (bf16[8,64,68]{2,0,1:T(8,128)(2,1)}, bf16[8,64,68]{2,0,1:T(8,128)(2,1)}, u32[]{:S(2)}, u32[]{:S(2)}) collective-permute-start(bf16[8,64,68]{2,0,1:T(8,128)(2,1)} %copy.758), channel_id=1, source_target_pairs={{0,1},{1,4},{4,5},{5,8},{8,9},{9,12},{12,13},{2,3},{3,6},{6,7},{7,... | collective-permute-start | bytes 208904 | tf_op jit(solution)/shard_map/ppermute | solution.py:22
  164.8 47.6 %reduce-scatter.21.cloned.1.call-start = ((), (), s32[]{:S(2)}) async-start(), calls=%async_computation.12 | async-start | bytes 98304
  166.8 3.9 %collective-permute-start.7 = (bf16[8,64,68]{2,0,1:T(8,128)(2,1)}, bf16[8,64,68]{2,0,1:T(8,128)(2,1)}, u32[]{:S(2)}, u32[]{:S(2)}) collective-permute-start(bf16[8,64,68]{2,0,1:T(8,128)(2,1)} %copy.758), channel_id=1, source_target_pairs={{1,0},{4,1},{5,4},{8,5},{9,8},{12,9},{13,12},{3,2},{6,3},{7,6},{10... | collective-permute-start | bytes 208904 | tf_op jit(solution)/shard_map/ppermute | solution.py:24
  169.6 49.6 %reduce-scatter.19.cloned.1.call-start = ((), (), s32[]{:S(2)}) async-start(), calls=%async_computation.11 | async-start | bytes 98304
  182.9 1.7 copy-start.30
  197.3 8.1 %copy-start.15 = (bf16[1,4,64,256]{3,2,1,0:T(8,128)(2,1)S(1)}, bf16[1,4,64,256]{3,2,1,0:T(8,128)(2,1)}, u32[]{:S(2)}) copy-start(bf16[1,4,64,256]{3,2,1,0:T(8,128)(2,1)} %copy.777) | copy-start | bytes 393220
  197.3 8.1 %copy-start.3 = (bf16[4,64,256]{2,1,0:T(8,128)(2,1)S(1)}, bf16[4,64,256]{2,1,0:T(8,128)(2,1)}, u32[]{:S(2)}) copy-start(bf16[4,64,256]{2,1,0:T(8,128)(2,1)} %copy-done.2) | copy-start | bytes 393220
  197.3 8.1 %copy-start.13 = (bf16[1,4,64,256]{3,2,1,0:T(8,128)(2,1)S(1)}, bf16[1,4,64,256]{3,2,1,0:T(8,128)(2,1)}, u32[]{:S(2)}) copy-start(bf16[1,4,64,256]{3,2,1,0:T(8,128)(2,1)} %copy.778) | copy-start | bytes 393220
  200.8 4.7 %copy-start.18 = (bf16[1,4,64,256]{3,2,1,0:T(8,128)(2,1)S(1)}, bf16[1,4,64,256]{3,2,1,0:T(8,128)(2,1)}, u32[]{:S(2)}) copy-start(bf16[1,4,64,256]{3,2,1,0:T(8,128)(2,1)} %copy.781) | copy-start | bytes 393220
  202.6 2.9 copy-start.22
  202.6 2.9 copy-start.20
  202.6 3.0 copy-start.8
  207.0 26.5 %reduce-scatter.17.cloned.1.call-start = ((), (), s32[]{:S(2)}) async-start(), calls=%async_computation.10 | async-start | bytes 393216 | tf_op jit(solution)/shard_map/reduce_scatter | solution.py:210
  208.5 38.9 %reduce-scatter.15.cloned.1.call-start = ((), (), s32[]{:S(2)}) async-start(), calls=%async_computation.9 | async-start | bytes 393216 | tf_op jit(solution)/shard_map/reduce_scatter | solution.py:210
  210.9 58.7 %all-reduce.7.cloned.1.call-start = ((), (), s32[]{:S(2)}) async-start(), calls=%async_computation.16 | async-start | bytes 1310720 | tf_op jit(solution)/shard_map/psum | solution.py:244
  212.4 57.2 %copy-start.11 = (bf16[4,256,256]{2,1,0:T(8,128)(2,1)S(1)}, bf16[4,256,256]{2,1,0:T(8,128)(2,1)}, u32[]{:S(2)}) copy-start(bf16[4,256,256]{2,1,0:T(8,128)(2,1)} %get-tuple-element.149) | copy-start | bytes 1572868
  212.4 57.2 %copy-start.28 = (bf16[2,256,64]{1,2,0:T(8,128)(2,1)S(1)}, bf16[2,256,64]{1,2,0:T(8,128)(2,1)}, u32[]{:S(2)}) copy-start(bf16[2,256,64]{1,2,0:T(8,128)(2,1)} %copy-done.26) | copy-start | bytes 196612
  249.2 65.4 %all-reduce.5.cloned.1.call-start = ((), (), s32[]{:S(2)}) async-start(), calls=%async_computation.15 | async-start | bytes 1310720 | tf_op jit(solution)/shard_map/psum | solution.py:243
Sparse Core Ops, SparseCore 0:
  108.4 13.9 reduce-scatter.24
  164.9 9.2 reduce-scatter.22
  177.0 9.8 reduce-scatter.20
  207.1 11.9 reduce-scatter.18
  221.8 11.6 reduce-scatter.16
  235.7 11.6 reduce-scatter.14
  250.5 19.0 all-reduce.6
  272.3 42.3 all-reduce.4
